TPU v7x, 256 devices: a whole 4x4x8 slice. The times are simulated.
256 devices in a mesh: row: 32 (over y, x, core), col: 8 (over z).
Axes of the slice: x: 4, y: 4, z: 8, core: 2. Of those that a mesh axis runs over, the one named last changes fastest.
Arguments:
- inputs: bfloat16 [4096, 6144], P('row', 'col'), may hold values from -6 to 6
- cotangent: bfloat16 [4096, 6144], P('row', 'col'), may hold values from -6 to 6
- saved_pre: bfloat16 [4096, 12288], P('col', 'row'), may hold values from -6 to 6
- weight_in: bfloat16 [6144, 12288], P('col', 'row'), may hold values from -0.078125 to 0.078125
- weight_out: bfloat16 [12288, 6144], P('row', 'col'), may hold values from -0.0546875 to 0.0546875
Outputs:
- input_grad: float32 [4096, 6144], P('row', 'col')
- weight_in_grad: float32 [6144, 12288], P('col', 'row')
- weight_out_grad: float32 [12288, 6144], P('row', 'col')
All inputs are finite; a program needn't handle non-finite values.
Results may differ from a plain program's by a relative error of at most 0.027.
Values may be sent and summed in bfloat16 or wider, within the bound.
No kernel may reach another device: no remote copies, remote signals or barrier semaphores. Data moves between devices by JAX's collectives and lax.ppermute only.
A program may use at most 128 MiB of HBM per device.

v0:
```python
import jax
import jax.numpy as jnp
from jax import lax
from jax.sharding import PartitionSpec as P

root_half = 0.7071067811865476
inverse_root = 0.3989422804014327


def gelu_parts(saved):
    widened = saved.astype(jnp.float32)
    lower_mass = 0.5 * (1.0 + lax.erf(widened * root_half))
    density = inverse_root * jnp.exp(-0.5 * widened * widened)
    return (widened * lower_mass, lower_mass + widened * density)


def body(inputs, cotangent, saved_pre, weight_in, weight_out):
    cot_rows = lax.all_gather(cotangent, "row", axis=0, tiled=True)
    picked = cot_rows
    hidden_grad = lax.psum_scatter(
        lax.dot_general(
            picked, weight_out, (((1,), (1,)), ((), ())), preferred_element_type=jnp.float32
        ).astype(jnp.bfloat16),
        "col",
        scatter_dimension=0,
        tiled=True,
    ).astype(jnp.float32)
    active, slope = gelu_parts(saved_pre)
    active_rows, grad_rows = (
        lax.all_gather(active.astype(jnp.bfloat16), "col", axis=0, tiled=True),
        lax.all_gather((hidden_grad * slope).astype(jnp.bfloat16), "col", axis=0, tiled=True),
    )
    out_grad = lax.dot_general(
        active_rows, cot_rows, (((0,), (0,)), ((), ())), preferred_element_type=jnp.float32
    )
    entry_grad = lax.dot_general(
        lax.all_gather(inputs, "row", axis=0, tiled=True),
        grad_rows,
        (((0,), (0,)), ((), ())),
        preferred_element_type=jnp.float32,
    )
    entry_grad, out_grad = (entry_grad, out_grad)
    picked = grad_rows
    token_grad = lax.psum_scatter(
        lax.dot_general(
            picked, weight_in, (((1,), (1,)), ((), ())), preferred_element_type=jnp.float32
        ).astype(jnp.bfloat16),
        "row",
        scatter_dimension=0,
        tiled=True,
    ).astype(jnp.float32)
    return (token_grad, entry_grad, out_grad)


def solution(mesh):
    in_specs = (P("row", "col"), P("row", "col"), P("col", "row"), P("col", "row"), P("row", "col"))
    out_specs = (P("row", "col"), P("col", "row"), P("row", "col"))
    return jax.shard_map(body, mesh=mesh, in_specs=in_specs, out_specs=out_specs, check_vma=False)
```

profile of v0, /device:TPU:2, one launch (start us, length us, event | category | flops | bytes accessed | tf_op | source)
XLA Modules:
  0.0 374.7 jit_solution(12998455347623308892)
XLA Ops:
  7.2 0.0 copy-start
  7.2 0.0 all-gather.5.cloned.1.call-start
  7.2 0.7 all-gather.5.cloned.1.call-update
  7.9 0.0 reduce-scatter.3.cloned.1.call-start
  8.0 59.0 %all-gather.5.cloned.1.call-done = bf16[4096,768]{1,0:T(8,128)(2,1)} async-done(((bf16[128,768]{1,0:T(8,128)(2,1)}), bf16[4096,768]{1,0:T(8,128)(2,1)}) %all-gather.5.cloned.1.call-update) | async-done | bytes 6291472 | tf_op jit(solution)/shard_map/all_gather | solution.py:18
  66.9 8.1 %convolution_convert_fusion.1 = bf16[4096,384]{1,0:T(8,128)(2,1)} fusion(bf16[4096,768]{1,0:T(8,128)(2,1)} %all-gather.5.cloned.1.call-done, bf16[384,768]{1,0:T(8,128)(2,1)} %param.9), kind=kOutput, calls=%fused_computation.1 | convolution fusion | flops 2417491968 | bytes 10027008 | tf_op jit(solution)/shard_map/dot_general | solution.py:21
  75.0 0.0 copy-start.1
  75.0 0.0 reduce-scatter.3.cloned.1.call-update
  75.0 0.0 all-gather.7.cloned.1.call-start
  75.1 46.7 %reduce-scatter.3.cloned.1.call-done = bf16[512,384]{1,0:T(8,128)(2,1)} async-done(((bf16[4096,384]{1,0:T(8,128)(2,1)}), bf16[512,384]{1,0:T(8,128)(2,1)}) %reduce-scatter.3.cloned.1.call-update) | async-done | bytes 393232 | tf_op jit(solution)/shard_map/reduce_scatter | solution.py:20
  121.7 0.0 copy-done.1
  121.7 2.3 fusion.8
  124.0 0.0 all-gather.7.cloned.1.call-update
  124.1 0.0 all-gather.9.cloned.1.call-start
  124.1 0.5 all-gather.9.cloned.1.call-update
  124.6 0.0 all-gather.11.cloned.1.call-start
  124.7 0.5 all-gather.11.cloned.1.call-update
  125.2 0.0 reduce-scatter.5.cloned.1.call-start
  125.3 43.2 %all-gather.7.cloned.1.call-done = bf16[4096,384]{1,0:T(8,128)(2,1)} async-done(((bf16[512,384]{1,0:T(8,128)(2,1)}), bf16[4096,384]{1,0:T(8,128)(2,1)}) %all-gather.7.cloned.1.call-update) | async-done | bytes 3145744 | tf_op jit(solution)/shard_map/all_gather | solution.py:31
  168.5 0.0 copy-done
  168.5 8.0 %convolution_convert_fusion = bf16[4096,768]{1,0:T(8,128)(2,1)} fusion(bf16[4096,384]{1,0:T(8,128)(2,1)} %all-gather.7.cloned.1.call-done, bf16[768,384]{1,0:T(8,128)(2,1)S(1)} %copy-done), kind=kOutput, calls=%fused_computation | convolution fusion | flops 2419064832 | bytes 10027008 | tf_op jit(solution)/shard_map/dot_general | solution.py:45
  176.5 0.0 reduce-scatter.5.cloned.1.call-update
  176.5 46.4 %all-gather.9.cloned.1.call-done = bf16[4096,768]{1,0:T(8,128)(2,1)} async-done(((bf16[128,768]{1,0:T(8,128)(2,1)}), bf16[4096,768]{1,0:T(8,128)(2,1)}) %all-gather.9.cloned.1.call-update) | async-done | bytes 6291472 | tf_op jit(solution)/shard_map/all_gather | solution.py:37
  223.0 6.4 %convolution_bitcast_fusion = f32[768,384]{0,1:T(8,128)S(1)} fusion(bf16[4096,384]{1,0:T(8,128)(2,1)} %all-gather.7.cloned.1.call-done, bf16[4096,768]{1,0:T(8,128)(2,1)} %all-gather.9.cloned.1.call-done), kind=kOutput, calls=%fused_computation.7 | convolution fusion | flops 2415919104 | bytes 10616832 | tf_op jit(solution)/shard_map/dot_general | solution.py:36
  229.3 1.4 copy.8
  230.7 39.2 %all-gather.11.cloned.1.call-done = bf16[4096,384]{1,0:T(8,128)(2,1)} async-done(((bf16[512,384]{1,0:T(8,128)(2,1)}), bf16[4096,384]{1,0:T(8,128)(2,1)}) %all-gather.11.cloned.1.call-update) | async-done | bytes 3145744 | tf_op jit(solution)/shard_map/all_gather | solution.py:30
  270.0 7.4 %fusion.9 = f32[384,768]{1,0:T(8,128)} fusion(bf16[4096,384]{1,0:T(8,128)(2,1)} %all-gather.11.cloned.1.call-done, bf16[4096,768]{1,0:T(8,128)(2,1)} %all-gather.5.cloned.1.call-done), kind=kOutput, calls=%fused_computation.17 | convolution fusion | flops 2415919104 | bytes 10616832 | tf_op jit(solution)/shard_map/dot_general | solution.py:33
  277.4 88.8 %reduce-scatter.5.cloned.1.call-done = bf16[128,768]{1,0:T(8,128)(2,1)} async-done(((bf16[4096,768]{1,0:T(8,128)(2,1)}), bf16[128,768]{1,0:T(8,128)(2,1)}) %reduce-scatter.5.cloned.1.call-update) | async-done | bytes 196624 | tf_op jit(solution)/shard_map/reduce_scatter | solution.py:44
  366.1 1.7 convert_element_type.26
Async XLA Ops:
  7.2 161.3 %copy-start = (bf16[768,384]{1,0:T(8,128)(2,1)S(1)}, bf16[768,384]{1,0:T(8,128)(2,1)}, u32[]{:S(2)}) copy-start(bf16[768,384]{1,0:T(8,128)(2,1)} %param.8) | copy-start | bytes 1769476
  7.2 59.8 %all-gather.5.cloned.1.call-start = ((), (), s32[]{:S(2)}) async-start(), calls=%async_computation.2 | async-start | bytes 6488064 | tf_op jit(solution)/shard_map/all_gather | solution.py:18
  7.9 113.8 %reduce-scatter.3.cloned.1.call-start = ((), (), s32[]{:S(2)}) async-start(), calls=%async_computation.3 | async-start | bytes 3538944 | tf_op jit(solution)/shard_map/reduce_scatter | solution.py:20
  75.0 46.7 %copy-start.1 = (bf16[512,384]{1,0:T(8,128)(2,1)S(1)}, bf16[512,384]{1,0:T(8,128)(2,1)}, u32[]{:S(2)}) copy-start(bf16[512,384]{1,0:T(8,128)(2,1)} %param.7) | copy-start | bytes 1179652
  75.0 93.5 %all-gather.7.cloned.1.call-start = ((), (), s32[]{:S(2)}) async-start(), calls=%async_computation.4 | async-start | bytes 3538944 | tf_op jit(solution)/shard_map/all_gather | solution.py:31
  124.1 98.9 %all-gather.9.cloned.1.call-start = ((), (), s32[]{:S(2)}) async-start(), calls=%async_computation.6 | async-start | bytes 6488064 | tf_op jit(solution)/shard_map/all_gather | solution.py:37
  124.6 145.3 %all-gather.11.cloned.1.call-start = ((), (), s32[]{:S(2)}) async-start(), calls=%async_computation.7 | async-start | bytes 3538944 | tf_op jit(solution)/shard_map/all_gather | solution.py:30
  125.2 240.9 %reduce-scatter.5.cloned.1.call-start = ((), (), s32[]{:S(2)}) async-start(), calls=%async_computation.5 | async-start | bytes 6488064 | tf_op jit(solution)/shard_map/reduce_scatter | solution.py:44
Sparse Core Ops, SparseCore 0:
  10.6 56.3 all-gather.4
  75.1 46.5 reduce-scatter.2
  124.2 44.2 all-gather.6
  170.9 52.0 all-gather.8
  225.2 44.7 all-gather.10
  273.8 92.2 reduce-scatter.4
where the time goes:
time: 375 us
  waiting for transfers between devices  325 us (87%)
  matrix products  29.8 us (8%)
  between operations  14.1 us (4%)
  other arithmetic  3.99 us (1%)
    reduce_scatter x1, waiting for transfers between devices, body(): lax.psum_scatter(lax.dot_general(picked, weight_in, (((1,), (1,)), ((), (...  88.8 us
    all_gather x1, waiting for transfers between devices, body(): cot_rows = lax.all_gather(cotangent, 'row', axis=0, tiled=True)  59 us
    reduce_scatter x1, waiting for transfers between devices, body(): lax.psum_scatter(lax.dot_general(picked, weight_out, (((1,), (1,)), ((),...  46.7 us
    all_gather x1, waiting for transfers between devices, body(): lax.all_gather(inputs, 'row', axis=0, tiled=True)  46.4 us
    all_gather x1, waiting for transfers between devices, body(): lax.all_gather((hidden_grad * slope).astype(jnp.bfloat16), 'col', axis=0,...  43.2 us
    all_gather x1, waiting for transfers between devices, body(): lax.all_gather(active.astype(jnp.bfloat16), 'col', axis=0, tiled=True)  39.2 us
    dot_general x1, matrix products, body(): lax.dot_general(picked, weight_out, (((1,), (1,)), ((), ())), preferred_e...  8.05 us
    dot_general x1, matrix products, body(): lax.dot_general(picked, weight_in, (((1,), (1,)), ((), ())), preferred_el...  8 us
  transfers between devices with their start and end apart: 6, of which 6 were waited for; matrix products, arithmetic and copies ran while one was open for 6% of the time, Pallas kernels for 0%

commit v1 on v0

v1 whole, which is shorter than its diff:
```python
import jax
import jax.numpy as jnp
from jax import lax
from jax.sharding import PartitionSpec as P

root_half = 0.7071067811865476
inverse_root = 0.3989422804014327
F32 = jnp.float32
BF16 = jnp.bfloat16

CORE_SWAP = [(r, r ^ 1) for r in range(32)]


def plane_pairs(k, first):
    pairs = []
    for r in range(32):
        y, x, core = r // 8, (r // 2) % 4, r % 2
        if (core == 0) == first:
            x ^= k
        else:
            y ^= k
        pairs.append((r, y * 8 + x * 2 + core))
    return pairs


def gelu_parts(saved):
    widened = saved.astype(F32)
    lower_mass = 0.5 * (1.0 + lax.erf(widened * root_half))
    density = inverse_root * jnp.exp(-0.5 * widened * widened)
    return (widened * lower_mass, lower_mass + widened * density)


def at(x, i):
    return lax.dynamic_index_in_dim(x, i, 0, keepdims=False)


def swap(x):
    return lax.ppermute(x, "row", CORE_SWAP)


def halves(shard, core):
    s, n, w = shard.shape
    split = shard.reshape(s, 2, n // 2, w)
    mine = lax.dynamic_index_in_dim(split, core, 1, keepdims=False)
    other = lax.dynamic_index_in_dim(split, 1 - core, 1, keepdims=False)
    return mine, other


def body(inputs, cotangent, saved_pre, weight_in, weight_out):
    row = lax.axis_index("row")
    y, x, core = row // 8, (row // 2) % 4, row % 2
    i1 = jnp.where(core == 0, x, y)
    i2 = jnp.where(core == 0, y, x)

    def flat(a2, a1):
        return jnp.where(core == 0, a2 * 4 + a1, a1 * 4 + a2)

    def both_shards(shard):
        mine, other = halves(shard[None], core)
        got = swap(other[0])
        pair = jnp.stack([mine[0], mine[0]])
        return lax.dynamic_update_index_in_dim(pair, got, 1 - core, 0)

    cot_pair = both_shards(cotangent)
    rows = cot_pair.shape[0] * cot_pair.shape[1]
    width = cot_pair.shape[2]
    cot_pair = cot_pair.reshape(rows, width)

    def plane_gather(block):
        first = [block] + [lax.ppermute(block, "row", plane_pairs(k, True)) for k in (1, 2, 3)]
        line = jnp.stack(first)
        second = [line] + [lax.ppermute(line, "row", plane_pairs(k, False)) for k in (1, 2, 3)]
        whole = jnp.zeros((16, rows, width), block.dtype)
        for k2 in range(4):
            for k1 in range(4):
                whole = lax.dynamic_update_index_in_dim(whole, second[k2][k1], flat(i2 ^ k2, i1 ^ k1), 0)
        return whole

    cot_all = plane_gather(cot_pair)

    out_weights = jnp.concatenate([weight_out, swap(weight_out)], 0)
    in_weights = jnp.concatenate([weight_in, swap(weight_in)], 1)
    hidden = out_weights.shape[0]

    saved_mine, saved_other = halves(saved_pre.reshape(4, -1, saved_pre.shape[1]), core)
    saved = jnp.concatenate([saved_mine, swap(saved_other)], 2).reshape(-1, hidden)
    active, slope = gelu_parts(saved)
    active_all = lax.all_gather(active.astype(BF16), "col", axis=0, tiled=True)

    hidden_grad = lax.psum_scatter(
        lax.dot_general(
            cot_all.reshape(-1, width), out_weights, (((1,), (1,)), ((), ())), preferred_element_type=F32
        ).astype(BF16),
        "col",
        scatter_dimension=0,
        tiled=True,
    ).astype(F32)

    same_core = [[r for r in range(32) if r % 2 == k] for k in (0, 1)]
    in_pair = both_shards(inputs).reshape(rows, width)
    in_all = lax.all_gather(in_pair, "row", axis=0, tiled=True, axis_index_groups=same_core)

    grad_all = lax.all_gather((hidden_grad * slope).astype(BF16), "col", axis=0, tiled=True)

    def weight_term(a, b, mine_axis):
        full = lax.dot_general(a, b, (((0,), (0,)), ((), ())), preferred_element_type=F32)
        mine, other = jnp.split(full, 2, mine_axis)
        return mine + swap(other)

    out_grad = weight_term(active_all, cot_all.reshape(-1, width), 0)

    token_grad = lax.dot_general(
        grad_all, in_weights, (((1,), (1,)), ((), ())), preferred_element_type=F32
    ).reshape(16, rows, width)
    token_bf = token_grad.astype(BF16)

    def pieces(k2):
        return jnp.stack([at(token_bf, flat(i2 ^ k2, i1 ^ k1)) for k1 in range(4)])

    line = pieces(0).astype(F32)
    for got in [lax.ppermute(pieces(k), "row", plane_pairs(k, False)) for k in (2, 1, 3)]:
        line = line + got.astype(F32)
    line_bf = line.astype(BF16)
    total = line[0]
    for got in [lax.ppermute(line_bf[k], "row", plane_pairs(k, True)) for k in (2, 1, 3)]:
        total = total + got.astype(F32)
    total = total.reshape(2, rows // 2, width)
    mine = at(total, core)
    got = swap(at(total, 1 - core))
    pair = lax.dynamic_update_index_in_dim(jnp.stack([mine, mine]), got, 1 - core, 0)
    entry_grad = weight_term(in_all, grad_all, 1)
    return (pair.reshape(rows, width), entry_grad, out_grad)


def solution(mesh):
    in_specs = (P("row", "col"), P("row", "col"), P("col", "row"), P("col", "row"), P("row", "col"))
    out_specs = (P("row", "col"), P("col", "row"), P("row", "col"))
    return jax.shard_map(body, mesh=mesh, in_specs=in_specs, out_specs=out_specs, check_vma=False)
```

time: 375 us -> 265 us (0.71)
  waiting for transfers between devices: 325 us -> 191 us
  starting transfers between devices: 0.24 us -> 18.6 us
  matrix products: 29.8 us -> 20.2 us
  other arithmetic: 3.99 us -> 11 us
  local copies, waits for them, and re-layouts: 1.4 us -> 7.42 us
    reduce_scatter x2 -> x1, waiting for transfers between devices: 135 us -> 43.5 us  [body(): lax.psum_scatter(lax.dot_general(cot_all.reshape(-1, width), out_weights,...]
    all_gather x4 -> x3, waiting for transfers between devices: 188 us -> 112 us  [the longest x1 40.4 us: body(): lax.all_gather(in_pair, 'row', axis=0, tiled=True, axis_index_groups=same...]
    ppermute x0 -> x20, waiting for transfers between devices: none -> 35.2 us  [the longest x3 21.1 us: plane_gather(): lax.ppermute(line, 'row', plane_pairs(k, False))]
    ppermute x0 -> x20, starting transfers between devices: none -> 18.5 us  [the longest x3 4.89 us: plane_gather(): lax.ppermute(line, 'row', plane_pairs(k, False))]
    dot_general x4, matrix products: 29.8 us -> 20.2 us  [the longest x2 10.2 us: weight_term(): lax.dot_general(a, b, (((0,), (0,)), ((), ())), preferred_element_type=F32)]
  transfers between devices with their start and end apart: 6 -> 24, of which waited for: 6 -> 15; matrix products, arithmetic and copies ran while one was open for 6% -> 11% of each run, Pallas kernels for 0% -> 0%
where the time goes in v1:
time: 265 us; the launch traced here: 263 us
  waiting for transfers between devices  191 us (72%)
  matrix products  20.2 us (8%)
  starting transfers between devices  18.6 us (7%)
  between operations  14.2 us (5%)
  other arithmetic  11 us (4%)
  local copies, waits for them, and re-layouts  7.42 us (3%)
    reduce_scatter x1, waiting for transfers between devices, body(): lax.psum_scatter(lax.dot_general(cot_all.reshape(-1, width), out_weights,...  43.5 us
    all_gather x1, waiting for transfers between devices, body(): lax.all_gather(in_pair, 'row', axis=0, tiled=True, axis_index_groups=same...  40.4 us
    all_gather x1, waiting for transfers between devices, body(): lax.all_gather((hidden_grad * slope).astype(BF16), 'col', axis=0, tiled=T...  38.4 us
    all_gather x1, waiting for transfers between devices, body(): active_all = lax.all_gather(active.astype(BF16), 'col', axis=0, tiled=True)  32.9 us
    ppermute x3, waiting for transfers between devices, plane_gather(): lax.ppermute(line, 'row', plane_pairs(k, False))  21.1 us
    dot_general x2, matrix products, weight_term(): lax.dot_general(a, b, (((0,), (0,)), ((), ())), preferred_element_type=F32)  10.2 us
    ppermute x8, waiting for transfers between devices, swap(): return lax.ppermute(x, 'row', CORE_SWAP)  7.5 us
    ppermute x3, waiting for transfers between devices, plane_gather(): lax.ppermute(block, 'row', plane_pairs(k, True))  6.65 us
  transfers between devices with their start and end apart: 24, of which 15 were waited for; matrix products, arithmetic and copies ran while one was open for 11% of the time, Pallas kernels for 0%

profile of v1, /device:TPU:2, one launch (start us, length us, event | category | flops | bytes accessed | tf_op | source)
XLA Modules:
  0.0 262.5 jit_solution(8763335074691941313)
XLA Ops:
  7.2 1.0 dynamic-slice_bitcast_fusion.4
  8.3 1.3 collective-permute-done
  9.6 2.4 collective-permute-start.1
  12.0 0.7 collective-permute-start.2
  12.6 0.9 collective-permute-start.3
  13.8 1.8 collective-permute-done.1
  15.6 3.6 %collective-permute-done.2 = bf16[128,768]{1,0:T(8,128)(2,1)S(1)} collective-permute-done((bf16[128,768]{1,0:T(8,128)(2,1)S(1)}, bf16[128,768]{1,0:T(8,128)(2,1)S(1)}, u32[]{:S(2)}, u32[]{:S(2)}) %collective-permute-start.2) | collective-permute-done | bytes 196640 | tf_op jit(solution)/shard_map/ppermute | solution.py:70
  19.2 1.2 collective-permute-done.3
  20.5 1.7 collective-permute-start.4
  22.2 0.3 broadcast_in_dim.39
  22.6 3.0 %collective-permute-start.5 = (bf16[4,128,768]{2,1,0:T(8,128)(2,1)S(1)}, bf16[4,128,768]{2,1,0:T(8,128)(2,1)S(1)}, u32[]{:S(2)}, u32[]{:S(2)}) collective-permute-start(bf16[4,128,768]{2,1,0:T(8,128)(2,1)S(1)} %pad_maximum_fusion), channel_id=1, source_target_pairs={{0,128},{8,40},{16,144},{24,56},{32,160},{40,8},{48,176},{56,24},{... | collective-permute-start | bytes 2359304 | tf_op jit(solution)/shard_map/ppermute | solution.py:72
  25.9 6.7 %collective-permute-done.4 = bf16[4,128,768]{2,1,0:T(8,128)(2,1)S(1)} collective-permute-done((bf16[4,128,768]{2,1,0:T(8,128)(2,1)S(1)}, bf16[4,128,768]{2,1,0:T(8,128)(2,1)S(1)}, u32[]{:S(2)}, u32[]{:S(2)}) %collective-permute-start.4) | collective-permute-done | bytes 786464 | tf_op jit(solution)/shard_map/ppermute | solution.py:72
  32.7 10.9 %collective-permute-done.5 = bf16[4,128,768]{2,1,0:T(8,128)(2,1)S(1)} collective-permute-done((bf16[4,128,768]{2,1,0:T(8,128)(2,1)S(1)}, bf16[4,128,768]{2,1,0:T(8,128)(2,1)S(1)}, u32[]{:S(2)}, u32[]{:S(2)}) %collective-permute-start.5) | collective-permute-done | bytes 786464 | tf_op jit(solution)/shard_map/ppermute | solution.py:72
  43.7 3.5 %collective-permute-done.6 = bf16[4,128,768]{2,1,0:T(8,128)(2,1)S(1)} collective-permute-done((bf16[4,128,768]{2,1,0:T(8,128)(2,1)S(1)}, bf16[4,128,768]{2,1,0:T(8,128)(2,1)S(1)}, u32[]{:S(2)}, u32[]{:S(2)}) %collective-permute-start.6) | collective-permute-done | bytes 786464 | tf_op jit(solution)/shard_map/ppermute | solution.py:72
  47.3 5.1 %convolution_convert_fusion.1 = bf16[2048,768]{1,0:T(8,128)(2,1)} fusion(bf16[2048,768]{1,0:T(8,128)(2,1)S(1)} %bitcast.61, bf16[384,768]{1,0:T(8,128)(2,1)} %collective-permute-done.7, bf16[384,768]{1,0:T(8,128)(2,1)S(1)} %copy-done.10), kind=kOutput, calls=%fused_computation.1 | convolution fusion | flops 2419851264 | bytes 7471104 | tf_op jit(solution)/shard_map/dot_general | solution.py:91
  52.5 1.1 constant_dynamic-slice_fusion.17
  53.6 1.4 collective-permute-done.8
  55.1 43.5 %reduce-scatter.2.cloned.1.call-done = bf16[256,768]{1,0:T(8,128)(2,1)} async-done(((bf16[2048,768]{1,0:T(8,128)(2,1)}), bf16[256,768]{1,0:T(8,128)(2,1)}) %reduce-scatter.2.cloned.1.call-update) | async-done | bytes 393232 | tf_op jit(solution)/shard_map/reduce_scatter | solution.py:90
  98.5 2.3 fusion.14
  100.9 0.7 all-gather.8.cloned.1.call-update
  101.6 1.0 dynamic-slice_bitcast_fusion.2
  102.7 1.3 collective-permute-done.17
  104.0 0.7 copy-done.8
  104.9 2.2 collective-permute-done.9
  107.1 38.4 %all-gather.4.cloned.1.call-done = bf16[2048,768]{1,0:T(8,128)(2,1)} async-done(((bf16[256,768]{1,0:T(8,128)(2,1)}), bf16[2048,768]{1,0:T(8,128)(2,1)}) %all-gather.4.cloned.1.call-update) | async-done | bytes 3145744 | tf_op jit(solution)/shard_map/all_gather | solution.py:103
  145.6 4.8 %convolution_convert_fusion = bf16[2048,768]{1,0:T(8,128)(2,1)S(1)} fusion(bf16[2048,768]{1,0:T(8,128)(2,1)} %all-gather.4.cloned.1.call-done, bf16[768,384]{1,0:T(8,128)(2,1)} %collective-permute-done.9, bf16[768,384]{1,0:T(8,128)(2,1)} %param.8), kind=kOutput, calls=%fused_computation | convolution fusion | flops 2419851264 | bytes 7471104 | tf_op jit(solution)/shard_map/dot_general | solution.py:112
  150.4 1.1 constant_dynamic-slice_fusion.16
  151.5 1.0 pad_maximum_fusion.1
  152.6 3.0 %collective-permute-start.10 = (bf16[4,128,768]{2,1,0:T(8,128)(2,1)}, bf16[4,128,768]{2,1,0:T(8,128)(2,1)}, u32[]{:S(2)}, u32[]{:S(2)}) collective-permute-start(bf16[4,128,768]{2,1,0:T(8,128)(2,1)} %pad_maximum_fusion.1), channel_id=1, source_target_pairs={{0,128},{8,40},{16,144},{24,56},{32,160},{40,8},{48,176},{56,24},{... | collective-permute-start | bytes 2359304 | tf_op jit(solution)/shard_map/ppermute | solution.py:121
  155.6 1.0 pad_maximum_fusion.2
  156.6 0.6 collective-permute-start.11
  157.1 1.0 pad_maximum_fusion.3
  158.1 0.6 collective-permute-start.12
  158.7 32.9 %all-gather.8.cloned.1.call-done = bf16[2048,768]{1,0:T(8,128)(2,1)} async-done(((bf16[256,768]{1,0:T(8,128)(2,1)}), bf16[2048,768]{1,0:T(8,128)(2,1)}) %all-gather.8.cloned.1.call-update) | async-done | bytes 3145744 | tf_op jit(solution)/shard_map/all_gather | solution.py:88
  191.6 4.7 %fusion.22 = f32[768,768]{1,0:T(8,128)S(1)} fusion(bf16[2048,768]{1,0:T(8,128)(2,1)} %all-gather.8.cloned.1.call-done, bf16[2048,768]{1,0:T(8,128)(2,1)S(1)} %bitcast.62), kind=kOutput, calls=%fused_computation.87 | convolution fusion | flops 2415919104 | bytes 8650752 | tf_op jit(solution)/shard_map/dot_general | solution.py:106
  196.3 1.2 split.19
  197.5 0.6 copy-done
  198.1 2.0 fusion.20
  200.2 2.2 collective-permute-start.13
  202.3 1.5 collective-permute-start.14
  203.8 0.6 collective-permute-start.15
  204.4 40.4 %all-gather.6.cloned.1.call-done = bf16[2048,768]{1,0:T(8,128)(2,1)} async-done(((bf16[128,768]{1,0:T(8,128)(2,1)}), bf16[2048,768]{1,0:T(8,128)(2,1)}) %all-gather.6.cloned.1.call-update) | async-done | bytes 3145744 | tf_op jit(solution)/shard_map/all_gather | solution.py:101
  244.8 5.6 %fusion.21 = f32[768,768]{1,0:T(8,128)S(1)} fusion(bf16[2048,768]{1,0:T(8,128)(2,1)} %all-gather.6.cloned.1.call-done, bf16[2048,768]{1,0:T(8,128)(2,1)} %all-gather.4.cloned.1.call-done), kind=kOutput, calls=%fused_computation.86 | convolution fusion | flops 2415919104 | bytes 8650752 | tf_op jit(solution)/shard_map/dot_general | solution.py:106
  250.6 1.2 fusion.17
  251.8 0.4 collective-permute-start.16
  252.3 1.3 collective-permute-done.16
  253.7 1.2 slice_add_fusion
  254.9 1.1 slice_add_fusion.1
  (70 shorter events, 2.0 us)
Async XLA Ops:
  7.2 91.4 %reduce-scatter.2.cloned.1.call-start = ((), (), s32[]{:S(2)}) async-start(), calls=%async_computation.1 | async-start | bytes 3538944 | tf_op jit(solution)/shard_map/reduce_scatter | solution.py:90
  8.2 1.4 collective-permute-start
  9.6 6.0 %collective-permute-start.1 = (bf16[128,768]{1,0:T(8,128)(2,1)S(1)}, bf16[128,768]{1,0:T(8,128)(2,1)S(1)}, u32[]{:S(2)}, u32[]{:S(2)}) collective-permute-start(bf16[128,768]{1,0:T(8,128)(2,1)S(1)} %bitcast.63), channel_id=1, source_target_pairs={{0,16},{8,72},{16,0},{24,88},{32,48},{40,104},{48,32},{56,120},{64... | collective-permute-start | bytes 589832 | tf_op jit(solution)/shard_map/ppermute | solution.py:70
  12.0 7.3 %collective-permute-start.2 = (bf16[128,768]{1,0:T(8,128)(2,1)S(1)}, bf16[128,768]{1,0:T(8,128)(2,1)S(1)}, u32[]{:S(2)}, u32[]{:S(2)}) collective-permute-start(bf16[128,768]{1,0:T(8,128)(2,1)S(1)} %bitcast.64), channel_id=1, source_target_pairs={{0,32},{8,136},{16,48},{24,152},{32,0},{40,168},{48,16},{56,184},{... | collective-permute-start | bytes 589832 | tf_op jit(solution)/shard_map/ppermute | solution.py:70
  12.6 7.8 %collective-permute-start.3 = (bf16[128,768]{1,0:T(8,128)(2,1)S(1)}, bf16[128,768]{1,0:T(8,128)(2,1)S(1)}, u32[]{:S(2)}, u32[]{:S(2)}) collective-permute-start(bf16[128,768]{1,0:T(8,128)(2,1)S(1)} %bitcast.65), channel_id=1, source_target_pairs={{0,48},{8,200},{16,32},{24,216},{32,16},{40,232},{48,0},{56,248},{... | collective-permute-start | bytes 589832 | tf_op jit(solution)/shard_map/ppermute | solution.py:70
  13.5 33.8 %collective-permute-start.7 = (bf16[384,768]{1,0:T(8,128)(2,1)}, bf16[384,768]{1,0:T(8,128)(2,1)}, u32[]{:S(2)}, u32[]{:S(2)}) collective-permute-start(bf16[384,768]{1,0:T(8,128)(2,1)} %param.9), channel_id=1, source_target_pairs={{0,8},{8,0},{16,24},{24,16},{32,40},{40,32},{48,56},{56,48},{64,72... | collective-permute-start | bytes 1769480 | tf_op jit(solution)/shard_map/ppermute | solution.py:38
  19.2 3.0 %copy-start.4 = (bf16[128,768]{1,0:T(8,128)(2,1)}, bf16[128,768]{1,0:T(8,128)(2,1)S(1)}, u32[]{:S(2)}) copy-start(bf16[128,768]{1,0:T(8,128)(2,1)S(1)} %collective-permute-done.2) | copy-start | bytes 589828
  20.4 1.8 copy-start.6
  20.5 12.1 %collective-permute-start.4 = (bf16[4,128,768]{2,1,0:T(8,128)(2,1)S(1)}, bf16[4,128,768]{2,1,0:T(8,128)(2,1)S(1)}, u32[]{:S(2)}, u32[]{:S(2)}) collective-permute-start(bf16[4,128,768]{2,1,0:T(8,128)(2,1)S(1)} %pad_maximum_fusion), channel_id=1, source_target_pairs={{0,64},{8,24},{16,80},{24,8},{32,96},{40,56},{48,112},{56,40},{64,... | collective-permute-start | bytes 2359304 | tf_op jit(solution)/shard_map/ppermute | solution.py:72
  22.2 3.6 %copy-start.5 = (bf16[128,768]{1,0:T(8,128)(2,1)S(1)}, bf16[128,768]{1,0:T(8,128)(2,1)}, u32[]{:S(2)}) copy-start(bf16[128,768]{1,0:T(8,128)(2,1)} %copy-done.4) | copy-start | bytes 589828
  22.2 3.7 %copy-start.7 = (bf16[128,768]{1,0:T(8,128)(2,1)S(1)}, bf16[128,768]{1,0:T(8,128)(2,1)}, u32[]{:S(2)}) copy-start(bf16[128,768]{1,0:T(8,128)(2,1)} %copy-done.6) | copy-start | bytes 589828
  22.5 24.8 %copy-start.10 = (bf16[384,768]{1,0:T(8,128)(2,1)S(1)}, bf16[384,768]{1,0:T(8,128)(2,1)}, u32[]{:S(2)}) copy-start(bf16[384,768]{1,0:T(8,128)(2,1)} %param.9) | copy-start | bytes 1769476
  22.6 21.0 %collective-permute-start.5 = (bf16[4,128,768]{2,1,0:T(8,128)(2,1)S(1)}, bf16[4,128,768]{2,1,0:T(8,128)(2,1)S(1)}, u32[]{:S(2)}, u32[]{:S(2)}) collective-permute-start(bf16[4,128,768]{2,1,0:T(8,128)(2,1)S(1)} %pad_maximum_fusion), channel_id=1, source_target_pairs={{0,128},{8,40},{16,144},{24,56},{32,160},{40,8},{48,176},{56,24},{... | collective-permute-start | bytes 2359304 | tf_op jit(solution)/shard_map/ppermute | solution.py:72
  25.5 21.6 %collective-permute-start.6 = (bf16[4,128,768]{2,1,0:T(8,128)(2,1)S(1)}, bf16[4,128,768]{2,1,0:T(8,128)(2,1)S(1)}, u32[]{:S(2)}, u32[]{:S(2)}) collective-permute-start(bf16[4,128,768]{2,1,0:T(8,128)(2,1)S(1)} %pad_maximum_fusion), channel_id=1, source_target_pairs={{0,192},{8,56},{16,208},{24,40},{32,224},{40,24},{48,240},{56,8},{... | collective-permute-start | bytes 2359304 | tf_op jit(solution)/shard_map/ppermute | solution.py:72
  52.4 93.2 %all-gather.4.cloned.1.call-start = ((), (), s32[]{:S(2)}) async-start(), calls=%async_computation.2 | async-start | bytes 3538944 | tf_op jit(solution)/shard_map/all_gather | solution.py:103
  53.5 1.5 collective-permute-start.8
  100.8 90.7 %all-gather.8.cloned.1.call-start = ((), (), s32[]{:S(2)}) async-start(), calls=%async_computation.4 | async-start | bytes 3538944 | tf_op jit(solution)/shard_map/all_gather | solution.py:88
  101.6 143.2 %all-gather.6.cloned.1.call-start = ((), (), s32[]{:S(2)}) async-start(), calls=%async_computation.3 | async-start | bytes 3342336 | tf_op jit(solution)/shard_map/all_gather | solution.py:101
  102.6 1.4 collective-permute-start.17
  104.0 0.7 copy-start.8
  104.7 2.4 collective-permute-start.9
  152.6 44.9 %collective-permute-start.10 = (bf16[4,128,768]{2,1,0:T(8,128)(2,1)}, bf16[4,128,768]{2,1,0:T(8,128)(2,1)}, u32[]{:S(2)}, u32[]{:S(2)}) collective-permute-start(bf16[4,128,768]{2,1,0:T(8,128)(2,1)} %pad_maximum_fusion.1), channel_id=1, source_target_pairs={{0,128},{8,40},{16,144},{24,56},{32,160},{40,8},{48,176},{56,24},{... | collective-permute-start | bytes 2359304 | tf_op jit(solution)/shard_map/ppermute | solution.py:121
  156.6 40.9 %collective-permute-start.11 = (bf16[4,128,768]{2,1,0:T(8,128)(2,1)}, bf16[4,128,768]{2,1,0:T(8,128)(2,1)}, u32[]{:S(2)}, u32[]{:S(2)}) collective-permute-start(bf16[4,128,768]{2,1,0:T(8,128)(2,1)} %pad_maximum_fusion.2), channel_id=1, source_target_pairs={{0,64},{8,24},{16,80},{24,8},{32,96},{40,56},{48,112},{56,40},{64,... | collective-permute-start | bytes 2359304 | tf_op jit(solution)/shard_map/ppermute | solution.py:121
  158.1 39.4 %collective-permute-start.12 = (bf16[4,128,768]{2,1,0:T(8,128)(2,1)}, bf16[4,128,768]{2,1,0:T(8,128)(2,1)}, u32[]{:S(2)}, u32[]{:S(2)}) collective-permute-start(bf16[4,128,768]{2,1,0:T(8,128)(2,1)} %pad_maximum_fusion.3), channel_id=1, source_target_pairs={{0,192},{8,56},{16,208},{24,40},{32,224},{40,24},{48,240},{56,8},{... | collective-permute-start | bytes 2359304 | tf_op jit(solution)/shard_map/ppermute | solution.py:121
  191.6 6.5 %copy-start.2 = (bf16[1,128,768]{2,1,0:T(8,128)(2,1)S(1)}, bf16[1,128,768]{2,1,0:T(8,128)(2,1)}, u32[]{:S(2)}) copy-start(bf16[1,128,768]{2,1,0:T(8,128)(2,1)} %get-tuple-element.19) | copy-start | bytes 589828
  191.6 6.5 %copy-start.3 = (bf16[1,128,768]{2,1,0:T(8,128)(2,1)S(1)}, bf16[1,128,768]{2,1,0:T(8,128)(2,1)}, u32[]{:S(2)}) copy-start(bf16[1,128,768]{2,1,0:T(8,128)(2,1)} %get-tuple-element.20) | copy-start | bytes 589828
  196.3 1.8 copy-start
  197.5 56.2 %collective-permute-start.19 = (f32[384,768]{1,0:T(8,128)}, f32[384,768]{1,0:T(8,128)S(1)}, u32[]{:S(2)}, u32[]{:S(2)}) collective-permute-start(f32[384,768]{1,0:T(8,128)} %split.19), channel_id=1, source_target_pairs={{0,8},{8,0},{16,24},{24,16},{32,40},{40,32},{48,56},{56,48},{64,72... | collective-permute-start | bytes 3538952 | tf_op jit(solution)/shard_map/ppermute | solution.py:38
  200.2 50.4 %collective-permute-start.13 = (bf16[128,768]{1,0:T(8,128)(2,1)S(1)}, bf16[128,768]{1,0:T(8,128)(2,1)S(1)}, u32[]{:S(2)}, u32[]{:S(2)}) collective-permute-start(bf16[128,768]{1,0:T(8,128)(2,1)S(1)} %get-tuple-element.21), channel_id=1, source_target_pairs={{0,32},{8,136},{16,48},{24,152},{32,0},{40,168},{48,16},{56,184},{... | collective-permute-start | bytes 589832 | tf_op jit(solution)/shard_map/ppermute | solution.py:125
  202.3 48.2 %collective-permute-start.14 = (bf16[128,768]{1,0:T(8,128)(2,1)S(1)}, bf16[128,768]{1,0:T(8,128)(2,1)}, u32[]{:S(2)}, u32[]{:S(2)}) collective-permute-start(bf16[128,768]{1,0:T(8,128)(2,1)S(1)} %get-tuple-element.23), channel_id=1, source_target_pairs={{0,16},{8,72},{16,0},{24,88},{32,48},{40,104},{48,32},{56,120},{64... | collective-permute-start | bytes 589832 | tf_op jit(solution)/shard_map/ppermute | solution.py:125
  203.8 46.7 %collective-permute-start.15 = (bf16[128,768]{1,0:T(8,128)(2,1)S(1)}, bf16[128,768]{1,0:T(8,128)(2,1)}, u32[]{:S(2)}, u32[]{:S(2)}) collective-permute-start(bf16[128,768]{1,0:T(8,128)(2,1)S(1)} %get-tuple-element.22), channel_id=1, source_target_pairs={{0,48},{8,200},{16,32},{24,216},{32,16},{40,232},{48,0},{56,248},{... | collective-permute-start | bytes 589832 | tf_op jit(solution)/shard_map/ppermute | solution.py:125
  250.3 3.4 %copy-start.1 = (f32[768,768]{1,0:T(8,128)S(1)}, f32[768,768]{1,0:T(8,128)}, u32[]{:S(2)}) copy-start(f32[768,768]{1,0:T(8,128)} %copy-done) | copy-start | bytes 7077892
  250.4 4.4 %collective-permute-start.18 = (f32[768,384]{1,0:T(8,128)S(1)}, f32[768,384]{1,0:T(8,128)S(1)}, u32[]{:S(2)}, u32[]{:S(2)}) collective-permute-start(f32[768,384]{1,0:T(8,128)S(1)} %split.17), channel_id=1, source_target_pairs={{0,8},{8,0},{16,24},{24,16},{32,40},{40,32},{48,56},{56,48},{64,72... | collective-permute-start | bytes 3538952 | tf_op jit(solution)/shard_map/ppermute | solution.py:38
  251.8 1.8 collective-permute-start.16
  253.7 2.3 copy-start.9
Sparse Core Ops, SparseCore 0:
  52.5 45.9 reduce-scatter.1
  101.0 44.5 all-gather.3
  147.9 43.6 all-gather.7
  193.9 50.8 all-gather.5
